TPU v7x, 512 devices: a whole 4x8x8 slice. The times are simulated.
512 devices in a mesh: band: 32 (over z_hi, y, core), frame: 16 (over x, z_lo).
Axes of the slice: x: 4, y: 8, z: 8 (z_hi: 2, z_lo: 4; z = z_hi * 4 + z_lo), core: 2. Of those that a mesh axis runs over, the one named last changes fastest.
Arguments:
- hidden: bfloat16 [32, 16, 256, 1152], P('band', 'frame'), may hold values from -6 to 6
- timesteps: int32 [32, 16], P('band', 'frame'), may hold values from 0 to 29
- ada_table: float32 [30, 3, 1152], replicated, may hold values from -3 to 3
- w_qkv: bfloat16 [1152, 3456], P('frame'), may hold values from -0.1875 to 0.1875
- w_out: bfloat16 [1152, 1152], P('frame'), may hold values from -0.1875 to 0.1875
- q_gain: float32 [72], replicated, may hold values from 0.5 to 2
- k_gain: float32 [72], replicated, may hold values from 0.5 to 2
- fresh: bfloat16 [256, 1152], replicated, may hold values from -6 to 6
Outputs:
- queue_next: bfloat16 [32, 16, 256, 1152], P('band', 'frame')
All inputs are finite; a program needn't handle non-finite values.
Results may differ from a plain program's by a relative error of at most 0.0095.
Values may be sent and summed in bfloat16 or wider, within the bound.
A program may use at most 64 MiB of HBM per device.

v0:
```python
import jax
import jax.numpy as jnp
from jax import lax
from jax.sharding import PartitionSpec as P


def shifted(block, axis, distance):
    devices = range(lax.axis_size(axis))
    route = [(i - distance, i) for i in devices if i - distance in devices]
    return lax.ppermute(block, axis, route)


def qk_norm(vec, gain):
    return vec * lax.rsqrt(jnp.mean(vec * vec, axis=-1, keepdims=True) + 1e-06) * gain


def rotate(vec, angle):
    half = vec.shape[-1] // 2
    first = vec[..., :half]
    second = vec[..., half:]
    cosine = jnp.cos(angle)
    sine = jnp.sin(angle)
    return jnp.concatenate(
        [first * cosine - second * sine, first * sine + second * cosine], axis=-1
    )


def add_rows(left, piece):
    return jnp.dot(left, piece, preferred_element_type=jnp.float32)


def project_qkv(rows_in, w_qkv):
    empty = jnp.zeros((rows_in.shape[0], w_qkv.shape[1]), jnp.float32)

    def fold_rows(total, piece, start):
        return add_rows(rows_in, piece)

    return fold_rows(empty, lax.all_gather(w_qkv, "frame", axis=0, tiled=True), jnp.int32(0))


def project_out(rows_in, w_out):
    empty = jnp.zeros((rows_in.shape[0], w_out.shape[1]), jnp.float32)

    def fold_rows(total, piece, start):
        return add_rows(rows_in, piece)

    return fold_rows(empty, lax.all_gather(w_out, "frame", axis=0, tiled=True), jnp.int32(0))


def finish_heads(qkv, position, q_gain, k_gain):
    count = qkv.shape[0]
    head_dim = q_gain.shape[0]
    width = qkv.shape[1] // 3
    heads = width // head_dim
    shaped = qkv.reshape(count, 3, heads, head_dim)
    half = head_dim // 2
    freq = jnp.power(10000.0, -2.0 * jnp.arange(half, dtype=jnp.float32) / head_dim)
    angle = position.astype(jnp.float32)[:, None, None] * freq
    query = rotate(qk_norm(shaped[:, 0], q_gain), angle).astype(jnp.bfloat16)
    keys = rotate(qk_norm(shaped[:, 1], k_gain), angle).astype(jnp.bfloat16)
    values = shaped[:, 2].astype(jnp.bfloat16)
    return (query, keys, values)


def attend(query, keys, values):
    head_dim = query.shape[-1]
    scores = jnp.einsum(
        "fnhd,gnhd->nhfg", query, keys, preferred_element_type=jnp.float32
    ) / jnp.sqrt(jnp.float32(head_dim))
    weights = jax.nn.softmax(scores, axis=-1).astype(jnp.bfloat16)
    return jnp.einsum(
        "nhfg,gnhd->fnhd", weights, values, preferred_element_type=jnp.float32
    ).astype(jnp.bfloat16)


def local(hidden, timesteps, ada_table, w_qkv, w_out, q_gain, k_gain, fresh):
    nframe = lax.axis_size("frame")
    frame_pos = lax.axis_index("frame")
    band_pos = lax.axis_index("band")
    rows = hidden.shape[2]
    width = hidden.shape[3]
    head_dim = q_gain.shape[0]
    heads = width // head_dim
    onehot = (jnp.arange(ada_table.shape[0], dtype=jnp.int32) == timesteps[0, 0]).astype(
        jnp.float32
    )
    modul = jnp.sum(onehot[:, None, None] * ada_table, axis=0)
    shift = modul[0][None, :]
    scale = modul[1][None, :]
    gate = modul[2][None, :]
    xf = hidden[0, 0].astype(jnp.float32)
    mean = jnp.mean(xf, axis=-1, keepdims=True)
    centred = xf - mean
    var = jnp.mean(centred * centred, axis=-1, keepdims=True)
    normed = (centred * lax.rsqrt(var + 1e-06) * (1.0 + scale) + shift).astype(jnp.bfloat16)
    qkv = project_qkv(normed, w_qkv)
    position = jnp.full((rows,), frame_pos, jnp.int32)
    query, keys, values = finish_heads(qkv, position, q_gain, k_gain)
    packed = jnp.stack(
        [query.reshape(rows, width), keys.reshape(rows, width), values.reshape(rows, width)], axis=1
    )[None]
    moved = lax.all_to_all(packed, "frame", split_axis=3, concat_axis=0, tiled=True)
    per_dev = heads // nframe
    moved = moved.reshape(nframe, rows, 3, per_dev, head_dim)
    attended = attend(moved[:, :, 0], moved[:, :, 1], moved[:, :, 2])
    attended = attended.reshape(nframe, rows, per_dev * head_dim)
    back = lax.all_to_all(attended, "frame", split_axis=0, concat_axis=2, tiled=True)
    delta = project_out(back[0], w_out)
    updated = (xf + gate * delta).astype(jnp.bfloat16)
    arrived = shifted(updated, ("band", "frame"), 1)
    first = jnp.logical_and(band_pos == 0, frame_pos == 0)
    result = jnp.where(first, fresh, arrived)
    return result[None, None]


def solution(mesh):
    return jax.shard_map(
        local,
        mesh=mesh,
        in_specs=(
            P("band", "frame", None, None),
            P("band", "frame"),
            P(),
            P("frame", None),
            P("frame", None),
            P(),
            P(),
            P(),
        ),
        out_specs=P("band", "frame", None, None),
        check_vma=False,
    )
```

profile of v0, /device:TPU:1, one launch (start us, length us, event | category | flops | bytes accessed | tf_op | source)
XLA Modules:
  0.0 395.5 jit_solution(734945233514541238)
XLA Ops:
  6.5 0.7 all-gather.3.cloned.1.call-update
  8.0 1.2 multiply_reduce_fusion.3
  9.7 185.2 %all-gather.3.cloned.1.call-done = bf16[1152,3456]{1,0:T(8,128)(2,1)} async-done(((bf16[72,3456]{1,0:T(8,128)(2,1)}), bf16[1152,3456]{1,0:T(8,128)(2,1)}) %all-gather.3.cloned.1.call-update) | async-done | bytes 7962640 | tf_op jit(solution)/shard_map/all_gather | solution.py:38
  194.9 11.4 %copy.16 = bf16[3456,1152]{1,0:T(8,128)(2,1)} copy(bf16[3456,1152]{0,1:T(8,128)(2,1)} %bitcast.84) | data formatting | bytes 15925248 | tf_op jit(solution)/shard_map/dot_general | solution.py:29
  206.3 5.9 %fusion.16 = f32[256,3,16,72]{0,3,2,1:T(8,128)S(1)} fusion(bf16[3,16,72,1152]{3,2,1,0:T(8,128)(2,1)} %bitcast.85, bf16[1,1,256,1152]{3,2,1,0:T(8,128)(2,1)S(1)} %copy-done, f32[1152]{0:T(1024)S(1)} %get-tuple-element.8, f32[1152]{0:T(1024)S(1)} %get-tuple-element.9, f32[256]{0:T(256)S(1)} %add_rsqrt_fusion.2, f32[256]{0:T(256)S(1)} %broadcast_multiply_fusion), kind=kOutput, calls=%fused_computation.39 | convolution fusion | flops 2040201216 | bytes 12102656 | tf_op jit(solution)/shard_map/dot_general | solution.py:29
  212.6 6.7 %copy.19 = bf16[256,1,1152]{0,1,2:T(2,128)(2,1)S(1)} copy(bf16[256,1,1152]{0,2,1:T(8,128)(2,1)S(1)} %bitcast.88) | data formatting | bytes 1179648 | tf_op jit(solution)/shard_map/convert_element_type | solution.py:61
  219.6 0.6 subtract_convert_fusion.1
  220.4 6.7 %copy.18 = bf16[256,1,1152]{0,1,2:T(2,128)(2,1)S(1)} copy(bf16[256,1,1152]{0,2,1:T(8,128)(2,1)S(1)} %bitcast.89) | data formatting | bytes 1179648 | tf_op jit(solution)/shard_map/convert_element_type | solution.py:60
  227.2 6.7 %copy.17 = bf16[256,1,1152]{0,1,2:T(2,128)(2,1)S(1)} copy(bf16[256,1,1152]{0,2,1:T(8,128)(2,1)S(1)} %bitcast.90) | data formatting | bytes 1179648 | tf_op jit(solution)/shard_map/convert_element_type | solution.py:59
  233.9 5.0 %maximum_bitcast_fusion = bf16[1,256,3,1152]{1,2,0,3:T(4,128)(2,1)} fusion(bf16[256,1,1152]{0,1,2:T(2,128)(2,1)S(1)} %copy.19, bf16[256,1,1152]{0,1,2:T(2,128)(2,1)S(1)} %copy.18, bf16[256,1,1152]{0,1,2:T(2,128)(2,1)S(1)} %copy.17), kind=kLoop, calls=%fused_computation.4 | loop fusion | flops 5308416 | bytes 3538944 | tf_op jit(solution)/shard_map/broadcast_in_dim | solution.py:99
  238.9 3.7 all-to-all-start
  242.7 0.7 all-gather.5.cloned.1.call-update
  243.4 93.0 %all-to-all-done = bf16[1,256,3,1152]{1,2,0,3:T(4,128)(2,1)S(1)} async-done(((bf16[1,256,3,1152]{1,2,0,3:T(4,128)(2,1)}), bf16[1,256,3,1152]{1,2,0,3:T(4,128)(2,1)S(1)}, u32[]{:S(2)}, u32[]{:S(2)}) %all-to-all-start) | async-done | bytes 1769504 | tf_op jit(solution)/shard_map/all_to_all | solution.py:102
  336.4 3.8 copy.21
  340.1 4.0 %fusion.26 = (f32[256,16]{1,0:T(8,128)S(1)}, f32[256,16,16]{1,2,0:T(8,128)}) fusion(bf16[16,256,3,1,72]{4,0,1,3,2:T(8,128)(2,1)} %bitcast.86), kind=kOutput, calls=%fused_computation.61 | convolution fusion | flops 9633807 | bytes 2375680 | tf_op jit(solution)/shard_map/sub | solution.py:70
  344.1 2.5 fusion.5
  346.6 1.5 copy.23
  348.1 4.9 %all-to-all-start.1 = ((bf16[16,256,72]{1,2,0:T(8,128)(2,1)}), bf16[16,256,72]{1,2,0:T(8,128)(2,1)S(1)}, u32[]{:S(2)}, u32[]{:S(2)}) async-start(bf16[16,256,72]{1,2,0:T(8,128)(2,1)} %copy.23), calls=%async_computation.1 | async-start | bytes 1179648 | tf_op jit(solution)/shard_map/all_to_all | solution.py:107
  353.0 1.5 all-gather.5.cloned.1.call-done
  354.5 15.3 %all-to-all-done.1 = bf16[16,256,72]{1,2,0:T(8,128)(2,1)S(1)} async-done(((bf16[16,256,72]{1,2,0:T(8,128)(2,1)}), bf16[16,256,72]{1,2,0:T(8,128)(2,1)S(1)}, u32[]{:S(2)}, u32[]{:S(2)}) %all-to-all-start.1) | async-done | bytes 589856 | tf_op jit(solution)/shard_map/all_to_all | solution.py:107
  369.8 2.8 fusion.2
  372.6 1.9 collective-permute-start
  374.6 13.2 %collective-permute-done = bf16[256,1152]{1,0:T(8,128)(2,1)S(1)} collective-permute-done((bf16[256,1152]{1,0:T(8,128)(2,1)S(1)}, bf16[256,1152]{1,0:T(8,128)(2,1)S(1)}, u32[]{:S(2)}, u32[]{:S(2)}) %collective-permute-start) | collective-permute-done | bytes 589856 | tf_op jit(solution)/shard_map/ppermute | solution.py:10
  387.8 0.9 select_bitcast_fusion
  (23 shorter events, 1.5 us)
Async XLA Ops:
  6.5 2.6 copy-start
  6.5 188.3 %all-gather.3.cloned.1.call-start = ((), (), s32[]{:S(2)}) async-start(), calls=%async_computation.2 | async-start | bytes 8460288 | tf_op jit(solution)/shard_map/all_gather | solution.py:38
  212.6 6.7 %copy-start.2 = (f32[72]{0:T(128)S(1)}, f32[72]{0:T(128)}, u32[]{:S(2)}) copy-start(f32[72]{0:T(128)} %param.13) | copy-start | bytes 868
  212.6 6.7 %copy-start.3 = (f32[72]{0:T(128)S(1)}, f32[72]{0:T(128)}, u32[]{:S(2)}) copy-start(f32[72]{0:T(128)} %param.14) | copy-start | bytes 868
  238.9 97.4 %all-to-all-start = ((bf16[1,256,3,1152]{1,2,0,3:T(4,128)(2,1)}), bf16[1,256,3,1152]{1,2,0,3:T(4,128)(2,1)S(1)}, u32[]{:S(2)}, u32[]{:S(2)}) async-start(bf16[1,256,3,1152]{1,2,0,3:T(4,128)(2,1)} %maximum_bitcast_fusion), calls=%async_computation | async-start | bytes 4718592 | tf_op jit(solution)/shard_map/all_to_all | solution.py:102
  242.7 111.8 %all-gather.5.cloned.1.call-start = ((), (), s32[]{:S(2)}) async-start(), calls=%async_computation.3 | async-start | bytes 2820096 | tf_op jit(solution)/shard_map/all_gather | solution.py:47
  348.1 21.7 %all-to-all-start.1 = ((bf16[16,256,72]{1,2,0:T(8,128)(2,1)}), bf16[16,256,72]{1,2,0:T(8,128)(2,1)S(1)}, u32[]{:S(2)}, u32[]{:S(2)}) async-start(bf16[16,256,72]{1,2,0:T(8,128)(2,1)} %copy.23), calls=%async_computation.1 | async-start | bytes 1179648 | tf_op jit(solution)/shard_map/all_to_all | solution.py:107
  369.8 18.0 %copy-start.1 = (bf16[256,1152]{1,0:T(8,128)(2,1)S(1)}, bf16[256,1152]{1,0:T(8,128)(2,1)}, u32[]{:S(2)}) copy-start(bf16[256,1152]{1,0:T(8,128)(2,1)} %param.15) | copy-start | bytes 1769476
  372.6 15.1 %collective-permute-start = (bf16[256,1152]{1,0:T(8,128)(2,1)S(1)}, bf16[256,1152]{1,0:T(8,128)(2,1)S(1)}, u32[]{:S(2)}, u32[]{:S(2)}) collective-permute-start(bf16[256,1152]{1,0:T(8,128)(2,1)S(1)} %fusion.2), channel_id=1, source_target_pairs={{0,1},{1,2},{2,3},{3,4},{4,5},{5,6},{6,7},{7,8},{8,9},{9,10},{10,1... | collective-permute-start | bytes 1769480 | tf_op jit(solution)/shard_map/ppermute | solution.py:10
Sparse Core Ops, SparseCore 0:
  9.4 185.3 all-gather.2
  245.6 108.8 all-gather.4
where the time goes:
time: 401 us; the launch traced here: 395 us
  waiting for transfers between devices  309 us (77%)
  local copies, waits for them, and re-layouts  36.8 us (9%)
  matrix products  15.2 us (4%)
  between operations  14.2 us (4%)
  starting transfers between devices  10.6 us (3%)
  other arithmetic  9.06 us (2%)
    all_gather x1, waiting for transfers between devices, project_qkv(): lax.all_gather(w_qkv, 'frame', axis=0, tiled=True)  185 us
    all_to_all x1, waiting for transfers between devices, local(): lax.all_to_all(packed, 'frame', split_axis=3, concat_axis=0, tiled=True)  93 us
    all_to_all x1, waiting for transfers between devices, local(): lax.all_to_all(attended, 'frame', split_axis=0, concat_axis=2, tiled=True)  15.3 us
    ppermute x1, waiting for transfers between devices, shifted(): return lax.ppermute(block, axis, route)  13.2 us
    dot_general x1, local copies, waits for them, and re-layouts, add_rows(): return jnp.dot(left, piece, preferred_element_type=jnp.float32)  11.4 us
    dot_general x2, matrix products, add_rows(): return jnp.dot(left, piece, preferred_element_type=jnp.float32)  8.79 us
  transfers between devices with their start and end apart: 5, of which 5 were waited for; matrix products, arithmetic and copies ran while one was open for 3% of the time, Pallas kernels for 0%

commit v1 on v0

v1 whole, which is shorter than its diff:
```python
import functools
import math

import jax
import jax.numpy as jnp
import numpy as np
from jax import lax
from jax.experimental import pallas as pl
from jax.experimental.pallas import tpu as pltpu
from jax.sharding import PartitionSpec as P

MESH = pl.DeviceIdType.MESH
D, HEADS, HD, ROWS, NF, STEPS, NB = 1152, 16, 72, 256, 16, 30, 32
TOK = ROWS // NF
F32, BF16 = jnp.float32, jnp.bfloat16
KMAIN, KREM = 1024, 256
KALL = 2 * KMAIN + 2 * KREM
V0, LO0, HI0 = KMAIN, 2 * KMAIN, 2 * KMAIN + KREM
OFFS = (0, -1, 1, 2)


def constants():
    source = np.full((KALL,), -1, np.int64)
    for c in range(2):
        for s in range(16):
            for r in range(32):
                source[c * 512 + s * 32 + r] = s * HD + c * 32 + r
    for m in range(2):
        for c in range(2):
            for s in range(16):
                for r in range(16):
                    source[V0 + (m * 2 + c) * 256 + s * 16 + r] = s * HD + c * 32 + m * 16 + r
    for s in range(16):
        for j in range(8):
            source[LO0 + s * 16 + j] = s * HD + 64 + j
            source[HI0 + s * 16 + 8 + j] = s * HD + 64 + j
    perm = np.zeros((D, KALL), np.float32)
    for n in range(KALL):
        if source[n] >= 0:
            perm[source[n], n] = 1.0
    lane = np.arange(D)
    gather = (lane[:, None] // HD == np.arange(128)[None, :]).astype(np.float32)
    spread = gather.T.copy()
    tile = (lane[None, :] % HD == np.arange(HD)[:, None]).astype(np.float32)
    half = HD // 2
    freq = np.power(10000.0, -2.0 * np.arange(half) / HD).astype(np.float32)
    angle = (np.arange(NF, dtype=np.float32)[:, None] * freq[None, :]).astype(np.float64)
    index = (lane % HD) % half
    first = (lane % HD) < half
    cosine = np.cos(angle)[:, index]
    sine = np.sin(angle)[:, index]
    rope = np.stack([cosine, np.where(first, -sine, 0.0), np.where(first, 0.0, sine)])
    rope = np.repeat(rope, 8, axis=1).astype(np.float32)
    masks = np.zeros((2, 4, 128, 384), np.float32)
    for g in range(2):
        for a in range(4):
            masks[g, a, :, 32 * a : 32 * a + 32] = 1.0
            masks[g, a, :, 128 + 32 * a : 128 + 32 * a + 32] = 1.0
            masks[g, a, :, 256 + 64 * g + 16 * a : 256 + 64 * g + 16 * a + 16] = 1.0
    masks = masks.reshape(2, 512, 384)
    return (
        jnp.asarray(perm, BF16),
        jnp.asarray(gather, BF16),
        jnp.asarray(spread, BF16),
        jnp.asarray(tile, F32),
        jnp.asarray(rope, F32),
        jnp.asarray(masks, BF16),
    )


def dot(a, b, **kw):
    return jnp.dot(a, b, preferred_element_type=F32, **kw)


def kernel(
    hidden, steps, table, wqkv, wout, q_gain, k_gain, perm_h, gather_h, spread_h, tile_h, rope_h, masks_h,
    out,
    eo, oc, wq_v, wo_v, x_v, table_v, tab, onehot, perm, gather, spread, tile, rope, masks, gain_v,
    modul, normed, xp, qf, rf, qb, kb, vb, vp, attp, delta, upd,
    send, recv, local, hsend, hrecv, osend, orecv, fsend, frecv,
):
    band = lax.axis_index("band")
    frame = lax.axis_index("frame")
    c = lax.rem(band, 2)
    y = lax.rem(band // 2, 8)
    par = lax.rem(y, 2)
    z_lo = lax.rem(frame, 4)
    x = frame // 4
    z = (band // 16) * 4 + z_lo

    def device(dx, dy, dz, core):
        xx = lax.rem(x + dx + 4, 4)
        yy = lax.rem(y + dy + 8, 8)
        zz = lax.rem(z + dz + 8, 8)
        return ((zz // 4) * 16 + yy * 2 + core, xx * 4 + lax.rem(zz, 4))

    a_up, a_dn = device(1 - c, 0, c, c), device(c - 1, 0, -c, c)
    b_up, b_dn = device(c, 0, 1 - c, c), device(-c, 0, c - 1, c)
    y_up, y_dn = device(0, 1, 0, c), device(0, -1, 0, c)
    sib = device(0, 0, 0, 1 - c)

    def shard(i, j):
        xx = lax.rem(x + i * (1 - c) + j * c + 4, 4)
        zz = lax.rem(z_lo + i * c + j * (1 - c) + 4, 4)
        return xx * 4 + zz

    def fetch(src, dst, k):
        cp = pltpu.make_async_copy(src, dst, local.at[k])
        cp.start()
        return cp

    got_w = [fetch(wqkv, wq_v, 0), fetch(wout, wo_v, 1)]
    own = pl.ds(pl.multiple_of(frame * TOK, TOK), TOK)
    got_own = fetch(hidden.at[own], x_v.at[own], 2)
    got_tab = fetch(table, table_v, 3)
    got_rest = [
        fetch(a, b, 4 + k)
        for k, (a, b) in enumerate(
            ((perm_h, perm), (gather_h, gather), (spread_h, spread), (tile_h, tile), (rope_h, rope), (masks_h, masks), (q_gain, gain_v.at[0]), (k_gain, gain_v.at[1]))
        )
    ]

    barrier = pltpu.get_barrier_semaphore()

    def greet(d):
        pl.semaphore_signal(barrier, inc=1, device_id=d, device_id_type=MESH)

    for d in (a_up, a_dn, b_up, b_dn, y_up, y_dn, sib):
        greet(d)
    for k in range(1, NF):
        greet((band, lax.rem(frame + k, NF)))

    @pl.when(jnp.logical_and(frame == 0, band > 0))
    def _():
        for k in range(NF):
            greet((band - 1, k))

    for cp in got_w:
        cp.wait()
    me = shard(0, 0)
    rest = wq_v[64:72, :].astype(F32)
    rest_o = wo_v[64:72, :].astype(F32)
    tails = (
        jnp.concatenate([rest[:, 0:D], rest[:, D : 2 * D]], axis=0).astype(BF16),
        jnp.concatenate([rest[:, 2 * D :], rest_o], axis=0).astype(BF16),
    )
    for cc in range(2):
        for m in range(2):
            eo[m, cc, me, 0:32, :] = wq_v[32 * cc : 32 * cc + 32, m * D : (m + 1) * D]
            eo[m, cc, me, 32:48, :] = wq_v[32 * cc + 16 * m : 32 * cc + 16 * m + 16, 2 * D :]
            eo[m, cc, me, 48:64, :] = tails[cc]
        oc[cc, me] = wo_v[32 * cc : 32 * cc + 32, :]

    pl.semaphore_wait(barrier, 22 + lax.min(NB - 1 - band, 1))

    pending = []

    def push(src, dst, d, rsem):
        k = len(pending)
        cp = pltpu.make_async_remote_copy(src, dst, send.at[k], recv.at[rsem], device_id=d, device_id_type=MESH)
        cp.start()
        pending.append(cp)

    def block(cls, i, j):
        if cls == "E":
            return eo.at[par, c, shard(i, j)]
        return oc.at[c, shard(i, j)]

    base = {"E": 0, "C": 16, "Y": 32, "SE": 48, "SC": 64, "SY": 80}

    def slot(kind, i, j):
        return base[kind] + (i + 1) * 4 + (j + 1)

    def push_block(cls, i, j, d, ri, rj):
        ref = block(cls, i, j)
        push(ref, ref, d, slot(cls, ri, rj))

    def expect(ref, rsem):
        pltpu.make_async_remote_copy(ref, ref, send.at[0], recv.at[rsem], device_id=sib, device_id_type=MESH).wait_recv()

    def start_own(cls):
        push_block(cls, 0, 0, b_up, 0, -1)
        push_block(cls, 0, 0, b_dn, 0, 1)
        push_block(cls, 0, 0, a_up, -1, 0)
        push_block(cls, 0, 0, a_dn, 1, 0)

    turn = [0]
    y_route = {}

    def take(cls, i, j):
        expect(block(cls, i, j), slot(cls, i, j))
        if j == 0:
            if cls == "E" and i == -1:
                push_block(cls, i, j, a_up, 2, 0)
            if cls == "C" and i == 1:
                push_block(cls, i, j, a_dn, 2, 0)
            push_block(cls, i, j, b_up, i, -1)
            push_block(cls, i, j, b_dn, i, 1)
        elif j == -1 and i in (0, -1):
            push_block(cls, i, j, b_up, i, 2)
        elif j == 1 and i in (1, 2):
            push_block(cls, i, j, b_dn, i, 2)
        ref = block(cls, i, j)
        if cls == "E":
            ycols = eo.at[par, c, shard(i, j), pl.ds(0, 48)]
            up = turn[0] % 2 == 0
            turn[0] += 1
            push(ycols, ycols, y_up if up else y_dn, slot("Y", i, j))
            y_route[(i, j)] = up
        push(ref, ref, sib, slot("S" + cls, i, j))

    def take_y(i, j):
        ref = eo.at[1 - par, c, shard(i, j), pl.ds(0, 48)]
        expect(ref, slot("Y", i, j))
        push(ref, ref, sib, slot("SY", i, j))

    ORDER = (
        (-1, 0), (1, 0), (0, -1), (0, 1), (2, 0),
        (-1, -1), (-1, 1), (1, 1), (1, -1), (2, 1), (2, -1),
        (0, 2), (-1, 2), (1, 2), (2, 2),
    )

    start_own("E")

    step = steps[0, 0]
    lanes = lax.broadcasted_iota(jnp.int32, (8, 128), 1)
    onehot[frame] = (lanes == step).astype(F32)
    h_copies = []
    for k in range(1, NF):
        to = lax.rem(frame + k, NF)
        rows = pl.ds(pl.multiple_of(to * TOK, TOK), TOK)
        h = pltpu.make_async_remote_copy(hidden.at[rows], x_v.at[own], hsend.at[k], hrecv.at[k], device_id=(band, to), device_id_type=MESH)
        o = pltpu.make_async_remote_copy(onehot.at[frame], onehot.at[frame], osend.at[k], orecv.at[k], device_id=(band, to), device_id_type=MESH)
        h.start()
        o.start()
        h_copies += [h, o]
    start_own("C")

    for i, j in ORDER[:5]:
        take("E", i, j)

    got_tab.wait()
    got_own.wait()
    for cp in got_rest:
        cp.wait()
    tab[...] = jnp.zeros_like(tab)
    for j in range(3):
        tab[j, 0:STEPS, :] = table_v[j]

    for i, j in ORDER[:5]:
        take("C", i, j)
    for i, j in ORDER[5:]:
        take("E", i, j)

    for k in range(1, NF):
        back = lax.rem(frame - k + NF, NF)
        rows = pl.ds(pl.multiple_of(back * TOK, TOK), TOK)
        pltpu.make_async_remote_copy(x_v.at[rows], x_v.at[rows], hsend.at[k], hrecv.at[k], device_id=sib, device_id_type=MESH).wait_recv()
        pltpu.make_async_remote_copy(onehot.at[back], onehot.at[back], osend.at[k], orecv.at[k], device_id=sib, device_id_type=MESH).wait_recv()

    oh = onehot[...].reshape(128, 128)
    for j in range(3):
        modul[j] = dot(oh, tab[j], precision=lax.Precision.HIGHEST)

    def norm_frame(f, _):
        r16 = pl.ds(pl.multiple_of(f * TOK, TOK), TOK)
        r8 = pl.multiple_of(f * 8, 8)
        v = x_v[r16, :].astype(F32)
        mean = jnp.mean(v, axis=-1, keepdims=True)
        cen = v - mean
        var = jnp.mean(cen * cen, axis=-1, keepdims=True)
        cen = cen * lax.rsqrt(var + 1e-06)
        scale = 1.0 + modul[1, pl.ds(r8, 8), :]
        shift = modul[0, pl.ds(r8, 8), :]
        normed[pl.ds(r8, 8), :] = cen[0:8] * scale + shift
        normed[pl.ds(pl.multiple_of(r8 + 128, 8), 8), :] = cen[8:16] * scale + shift
        return 0

    lax.fori_loop(0, NF, norm_frame, 0, unroll=4)
    qb[...] = normed[...].astype(BF16)

    def permute(n, _):
        cols = pl.ds(pl.multiple_of(n * 512, 512), 512)
        xp[:, cols] = dot(qb[...], perm[:, cols]).astype(BF16)
        return 0

    lax.fori_loop(0, KALL // 512, permute, 0)

    for i, j in ORDER[5:]:
        take("C", i, j)
    for i, j in ORDER:
        take_y(i, j)
    for i, j in ORDER:
        ref = eo.at[par, 1 - c, shard(i, j)]
        expect(ref, slot("SE", i, j))
    for i, j in ORDER:
        ref = eo.at[1 - par, 1 - c, shard(i, j), pl.ds(0, 48)]
        expect(ref, slot("SY", i, j))

    NT = 384

    def project(dst, pieces):
        def one(n, _):
            cols = pl.ds(pl.multiple_of(n * NT, NT), NT)
            total = None
            for lhs, rhs in pieces:
                term = dot(lhs(), rhs(cols))
                total = term if total is None else total + term
            dst[:, cols] = total.astype(dst.dtype)
            return 0

        lax.fori_loop(0, D // NT, one, 0)

    def lhs_at(ref, start, width):
        return lambda: ref[:, start : start + width]

    def rhs_at(m, cc, lo, n):
        return lambda cols: eo[m, cc, :, lo : lo + n, cols].reshape(16 * n, NT)

    def heads_of(m, dst):
        project(qf, [
            (lhs_at(xp, 0, 512), rhs_at(m, 0, 0, 32)),
            (lhs_at(xp, 512, 512), rhs_at(m, 1, 0, 32)),
            (lhs_at(xp, LO0 if m == 0 else HI0, KREM), rhs_at(par, 0, 48, 16)),
        ])
        squares = qf[...]
        ss = dot((squares * squares).astype(BF16), gather[...])
        r = lax.rsqrt(ss * (1.0 / HD) + 1e-06)
        hi = r.astype(BF16)
        lo = (r - hi.astype(F32)).astype(BF16)
        rf[...] = dot(hi, spread[...]) + dot(lo, spread[...])
        gain = dot(jnp.broadcast_to(gain_v[m], (8, HD)), tile[...], precision=lax.Precision.HIGHEST)[0:1, :]

        def turn_rows(g, _):
            r32 = pl.ds(pl.multiple_of(g * 32, 32), 32)
            t32 = pl.ds(pl.multiple_of(lax.rem(g, 4) * 32, 32), 32)
            v = qf[r32, :] * rf[r32, :] * gain
            w = v * rope[0, t32, :]
            w = w + pltpu.roll(v, D - HD // 2, 1) * rope[1, t32, :]
            w = w + pltpu.roll(v, HD // 2, 1) * rope[2, t32, :]
            dst[r32, :] = w.astype(BF16)
            return 0

        lax.fori_loop(0, ROWS // 32, turn_rows, 0)

    heads_of(0, qb)
    heads_of(1, kb)
    project(vb, [
        (lhs_at(xp, V0 + (m * 2 + cc) * 256, 256), rhs_at(m, cc, 32, 16)) for m in range(2) for cc in range(2)
    ] + [(lhs_at(xp, LO0, KREM), rhs_at(par, 1, 48, 16))])
    vp[:, 0:512] = dot(vb[...], perm[:, 0:512]).astype(BF16)
    vp[:, 512:1024] = dot(vb[...], perm[:, 512:1024]).astype(BF16)
    vp[:, 1024:1280] = dot(vb[...], perm[:, HI0:KALL]).astype(BF16)

    same = (
        lax.rem(lax.broadcasted_iota(jnp.int32, (128, 128), 0), 8)
        == lax.rem(lax.broadcasted_iota(jnp.int32, (128, 128), 1), 8)
    ).astype(F32)
    factor = 1.0 / math.sqrt(HD)

    def attend(h, _):
        rows = pl.ds(pl.multiple_of(h * 128, 128), 128)
        num_rem = den_rem = None
        for g in range(4):
            probs = []
            for a in range(4):
                hd = 4 * g + a
                w = (HD * hd) // 128 * 128
                width = min(256, D - w)
                lane = lax.broadcasted_iota(jnp.int32, (16, width), 1) + w
                pick = jnp.logical_and(lane >= HD * hd, lane < HD * (hd + 1)).astype(F32).astype(BF16)
                pick = jnp.concatenate([pick] * 8, axis=0)
                kw = kb[rows, w : w + width] * pick
                sc = lax.dot_general(qb[rows, w : w + width], kw, (((1,), (1,)), ((), ())), preferred_element_type=F32)
                probs.append((jnp.exp(sc * factor) * same).astype(BF16))
            p4 = jnp.concatenate(probs, axis=1)
            vg = jnp.concatenate([
                vp[rows, g * 128 : g * 128 + 128],
                vp[rows, 512 + g * 128 : 512 + g * 128 + 128],
                vp[rows, 1024 + (g // 2) * 128 : 1024 + (g // 2) * 128 + 128],
            ], axis=1)
            mk = masks[g % 2]
            num = dot(p4, jnp.concatenate([vg] * 4, axis=0) * mk)
            den = dot(p4, mk)
            inv = 1.0 / den[:, 0:128]
            attp[rows, g * 128 : g * 128 + 128] = (num[:, 0:128] * inv).astype(BF16)
            attp[rows, 512 + g * 128 : 512 + g * 128 + 128] = (num[:, 128:256] * inv).astype(BF16)
            if g % 2 == 0:
                num_rem, den_rem = num[:, 256:384], den[:, 256:384]
            else:
                lo = 1024 + (g // 2) * 128
                attp[rows, lo : lo + 128] = ((num_rem + num[:, 256:384]) / (den_rem + den[:, 256:384])).astype(BF16)
        return 0

    lax.fori_loop(0, 2, attend, 0)

    for i, j in ORDER:
        expect(oc.at[1 - c, shard(i, j)], slot("SC", i, j))

    project(delta, [
        (lhs_at(attp, 0, 512), lambda cols: oc[0, :, :, cols].reshape(512, NT)),
        (lhs_at(attp, 512, 512), lambda cols: oc[1, :, :, cols].reshape(512, NT)),
        (lhs_at(attp, 1024, KREM), rhs_at(par, 1, 48, 16)),
    ])

    f_copies = []
    for k in range(NF):
        f = lax.rem(frame + k, NF)
        r16 = pl.ds(pl.multiple_of(f * TOK, TOK), TOK)
        r8 = pl.multiple_of(f * 8, 8)
        gate = modul[2, pl.ds(r8, 8), :]
        both = jnp.concatenate([
            gate * delta[pl.ds(r8, 8), :],
            gate * delta[pl.ds(pl.multiple_of(r8 + 128, 8), 8), :],
        ], axis=0)
        upd[r16, :] = (x_v[r16, :].astype(F32) + both).astype(BF16)
        last = f // (NF - 1)
        to_band = band + last
        to_frame = lax.rem(f + 1, NF)
        cp = pltpu.make_async_remote_copy(upd.at[r16], out.at[own], fsend.at[k], frecv.at[frame], device_id=(to_band, to_frame), device_id_type=MESH)
        here = jnp.logical_and(to_band == band, to_frame == frame)
        inside = to_band < NB
        if k < NF - 1:
            pl.when(inside)(cp.start)
            f_copies.append((inside, cp))
        else:
            away = jnp.logical_and(inside, frame == 0)
            pl.when(away)(cp.start)
            f_copies.append((away, cp))
            stay = pltpu.make_async_copy(upd.at[r16], out.at[own], local.at[0])

            @pl.when(frame > 0)
            def _():
                stay.start()
                stay.wait()

    def arrive(f):
        rows = pl.ds(pl.multiple_of(f * TOK, TOK), TOK)
        pltpu.make_async_remote_copy(out.at[rows], out.at[rows], fsend.at[0], frecv.at[f], device_id=sib, device_id_type=MESH).wait_recv()

    for f in range(NF):
        comes = jnp.logical_or(jnp.logical_and(frame > 0, frame != f), jnp.logical_and(frame == 0, band > 0))
        pl.when(comes)(functools.partial(arrive, f))

    for cond, cp in f_copies:
        pl.when(cond)(cp.wait_send)
    for cp in h_copies:
        cp.wait_send()
    for cp in pending:
        cp.wait_send()


def local_step(hidden, timesteps, ada_table, w_qkv, w_out, q_gain, k_gain, fresh):
    hbm = pl.BlockSpec(memory_space=pl.ANY)
    consts = constants()
    shapes = [
        pltpu.VMEM((2, 2, 16, 64, D), BF16),
        pltpu.VMEM((2, 16, 32, D), BF16),
        pltpu.VMEM((72, 3 * D), BF16),
        pltpu.VMEM((72, D), BF16),
        pltpu.VMEM((ROWS, D), BF16),
        pltpu.VMEM((3, STEPS, D), F32),
        pltpu.VMEM((3, 128, D), F32),
        pltpu.VMEM((NF, 8, 128), F32),
        *[pltpu.VMEM(a.shape, a.dtype) for a in consts],
        pltpu.VMEM((2, 1, HD), F32),
        pltpu.VMEM((3, 128, D), F32),
        pltpu.VMEM((ROWS, D), F32),
        pltpu.VMEM((ROWS, KALL), BF16),
        pltpu.VMEM((ROWS, D), F32),
        pltpu.VMEM((ROWS, D), F32),
        pltpu.VMEM((ROWS, D), BF16),
        pltpu.VMEM((ROWS, D), BF16),
        pltpu.VMEM((ROWS, D), BF16),
        pltpu.VMEM((ROWS, 1280), BF16),
        pltpu.VMEM((ROWS, 1280), BF16),
        pltpu.VMEM((ROWS, D), F32),
        pltpu.VMEM((ROWS, D), BF16),
        pltpu.SemaphoreType.DMA((96,)),
        pltpu.SemaphoreType.DMA((96,)),
        pltpu.SemaphoreType.DMA((12,)),
        *[pltpu.SemaphoreType.DMA((NF,)) for _ in range(6)],
    ]
    moved = pl.pallas_call(
        kernel,
        out_shape=jax.ShapeDtypeStruct((ROWS, D), BF16),
        in_specs=[hbm, pl.BlockSpec(memory_space=pltpu.SMEM)] + [hbm] * (5 + len(consts)),
        out_specs=hbm,
        scratch_shapes=shapes,
        compiler_params=pltpu.CompilerParams(collective_id=0, has_side_effects=True, vmem_limit_bytes=56 << 20),
        name="queue_step",
    )(hidden[0, 0], timesteps, jnp.transpose(ada_table, (1, 0, 2)), w_qkv, w_out, q_gain[None], k_gain[None], *consts)
    first = jnp.logical_and(lax.axis_index("band") == 0, lax.axis_index("frame") == 0)
    return jnp.where(first, fresh, moved)[None, None]


def solution(mesh):
    return jax.shard_map(
        local_step,
        mesh=mesh,
        in_specs=(
            P("band", "frame", None, None),
            P("band", "frame"),
            P(),
            P("frame", None),
            P("frame", None),
            P(),
            P(),
            P(),
        ),
        out_specs=P("band", "frame", None, None),
        check_vma=False,
    )
```

time: 401 us -> 87.2 us (0.22); the launches traced: 395 us -> 86.9 us
  waiting for transfers between devices: 309 us -> 0 us
  Pallas kernels: 0 us -> 84.3 us
  local copies, waits for them, and re-layouts: 36.8 us -> 0.01 us
  matrix products: 15.2 us -> 0 us
  between operations: 14.2 us -> 0.73 us
  starting transfers between devices: 10.6 us -> 0 us
  other arithmetic: 9.06 us -> 1.96 us
    all_gather x2 -> x0, waiting for transfers between devices: 187 us -> none  [the longest x1 185 us: project_qkv(): lax.all_gather(w_qkv, 'frame', axis=0, tiled=True)]
    all_to_all x2 -> x0, waiting for transfers between devices: 108 us -> none  [the longest x1 93 us: local(): lax.all_to_all(packed, 'frame', split_axis=3, concat_axis=0, tiled=True)]
    pallas_call x0 -> x1, Pallas kernels: none -> 84.3 us  [local_step(): pl.pallas_call(kernel, out_shape=jax.ShapeDtypeStruct((ROWS, D), BF16), i...]
    convert_element_type x3 -> x0, local copies, waits for them, and re-layouts: 20 us -> none  [the longest x1 6.68 us: finish_heads(): values = shaped[:, 2].astype(jnp.bfloat16)]
    ppermute x1 -> x0, waiting for transfers between devices: 13.2 us -> none  [shifted(): return lax.ppermute(block, axis, route)]
    dot_general x1 -> x0, local copies, waits for them, and re-layouts: 11.4 us -> none  [add_rows(): return jnp.dot(left, piece, preferred_element_type=jnp.float32)]
    dot_general x3 -> x0, matrix products: 11.2 us -> none  [the longest x2 8.79 us: add_rows(): return jnp.dot(left, piece, preferred_element_type=jnp.float32)]
    all_to_all x2 -> x0, starting transfers between devices: 8.63 us -> none  [the longest x1 4.91 us: local(): lax.all_to_all(attended, 'frame', split_axis=0, concat_axis=2, tiled=True)]
  transfers between devices with their start and end apart: 5 -> 0, of which waited for: 5 -> 0; matrix products, arithmetic and copies ran while one was open for 3% -> 0% of each run, Pallas kernels for 0% -> 0%
where the time goes in v1:
time: 87.2 us; the launch traced here: 86.9 us
  Pallas kernels  84.3 us (97%)
  other arithmetic  1.96 us (2%)
    pallas_call x1, Pallas kernels, local_step(): pl.pallas_call(kernel, out_shape=jax.ShapeDtypeStruct((ROWS, D), BF16), i...  84.3 us
    broadcast_in_dim x1, other arithmetic, local_step(): return jnp.where(first, fresh, moved)[None, None]  1.96 us

profile of v1, /device:TPU:1, one launch (start us, length us, event | category | flops | bytes accessed | tf_op | source)
XLA Modules:
  0.0 86.9 jit_solution(12207735749074598126)
XLA Ops:
  0.0 0.0 copy-start
  0.7 84.3 %queue_step.1 = bf16[256,1152]{1,0:T(8,128)(2,1)} custom-call(bf16[256,1152]{1,0:T(8,128)(2,1)} %bitcast.6, s32[1,1]{1,0:T(1,128)S(6)} %copy.15.steps, f32[3,30,1152]{2,1,0:T(8,128)} %bitcast.7, bf16[72,3456]{1,0:T(8,128)(2,1)} %wqkv.1, bf16[72,1152]{1,0:T(8,128)(2,1)} %wout.1, f32[1,72]{1,0:T(1,128)} %bitcast.8, f32[1,72]{1,0:T(1,128)} %bitcast.9, ...), custom_call_target="tpu_custom_call" | custom-call | tf_op jit(solution)/shard_map/queue_step/pallas_call | solution.py:484
  85.0 0.0 copy-done
  85.0 2.0 %select_bitcast_fusion = bf16[1,1,256,1152]{3,2,1,0:T(8,128)(2,1)} fusion(bf16[256,1152]{1,0:T(8,128)(2,1)S(1)} %copy-done, bf16[256,1152]{1,0:T(8,128)(2,1)} %queue_step.1, pred[]{:T(512)S(6)} %and.5), kind=kLoop, calls=%fused_computation | loop fusion | flops 294912 | bytes 1769473 | tf_op jit(solution)/shard_map/broadcast_in_dim | solution.py:494
Async XLA Ops:
  0.0 85.0 %copy-start = (bf16[256,1152]{1,0:T(8,128)(2,1)S(1)}, bf16[256,1152]{1,0:T(8,128)(2,1)}, u32[]{:S(2)}) copy-start(bf16[256,1152]{1,0:T(8,128)(2,1)} %param.21) | copy-start | bytes 1769476

commit v2 on v1

v2 whole, which is shorter than its diff:
```python
import functools
import math

import jax
import jax.numpy as jnp
import numpy as np
from jax import lax
from jax.experimental import pallas as pl
from jax.experimental.pallas import tpu as pltpu
from jax.sharding import PartitionSpec as P

MESH = pl.DeviceIdType.MESH
D, HEADS, HD, ROWS, NF, STEPS, NB = 1152, 16, 72, 256, 16, 30, 32
TOK = ROWS // NF
F32, BF16 = jnp.float32, jnp.bfloat16
KMAIN, KREM = 1024, 256
LO0, HI0, O0 = KMAIN, KMAIN + KREM, KMAIN + 2 * KREM
KALL = O0 + KMAIN
KINDS = ("E", "F", "C", "YE", "YF", "YC")
WORK = ("tab", "mod", "rope", "ln", "p0", "p1", "p2", "f0", "f1", "f2", "g0", "g1", "g2", "v", "vp", "a0", "a1")
HOPS = (
    ((-1, 0), (1, 0), (0, -1), (0, 1)),
    ((2, 0), (-1, -1), (-1, 1), (1, 1), (1, -1), (0, 2)),
    ((2, 1), (2, -1), (-1, 2), (1, 2)),
    ((2, 2),),
)
SCHEDULE = (
    ("E", -1), (3, 0), ("F", -1), ("C", -1), ("E", 0, 1), ("tab", 0), ("mod", 0), ("rope", 0),
    ("F", 0), ("C", 0), ("E", 1, 1), ("F", 1), ("C", 1), ("E", 2, 1), ("YE", 0), ("F", 2),
    ("C", 2), ("E", 3), ("YE", 1), ("F", 3), ("ln", 0), ("YE", 2), ("p0", 0), ("YF", 0),
    ("YF", 1), ("YC", 0), ("p1", 0), ("YE", 3), ("p2", 0), ("C", 3), ("f0", 0), ("YF", 2),
    ("YF", 3), ("f1", 0), ("f2", 0), ("YC", 1), ("g0", 0), ("g1", 0), ("g2", 0), ("YC", 2),
    ("v", 0), ("YC", 3), ("vp", 0), ("a0", 0), ("a1", 0),
)


def constants():
    source = np.full((KALL,), -1, np.int64)
    for c in range(2):
        for s in range(16):
            for r in range(32):
                source[O0 + c * 512 + s * 32 + r] = s * HD + c * 32 + r
    for m in range(2):
        for c in range(2):
            for s in range(16):
                for r in range(16):
                    source[(m * 2 + c) * 256 + s * 16 + r] = s * HD + c * 32 + m * 16 + r
    for s in range(16):
        for j in range(8):
            source[LO0 + s * 16 + j] = s * HD + 64 + j
            source[HI0 + s * 16 + 8 + j] = s * HD + 64 + j
    perm = np.zeros((D, KALL), np.float32)
    for n in range(KALL):
        if source[n] >= 0:
            perm[source[n], n] = 1.0
    lane = np.arange(D)
    gather = (lane[:, None] // HD == np.arange(128)[None, :]).astype(np.float32)
    spread = gather.T.copy()
    tile = (lane[None, :] % HD == np.arange(HD)[:, None]).astype(np.float32)
    half = HD // 2
    freq = np.power(10000.0, -2.0 * np.arange(half) / HD).astype(np.float32)
    angle = (np.arange(NF, dtype=np.float32)[:, None] * freq[None, :]).astype(np.float64)
    index = (lane % HD) % half
    first = (lane % HD) < half
    cosine = np.cos(angle)[:, index]
    sine = np.sin(angle)[:, index]
    rope = np.stack([cosine, np.where(first, -sine, 0.0), np.where(first, 0.0, sine)])
    rope = np.repeat(rope, 8, axis=1).astype(np.float32)
    masks = np.zeros((2, 4, 128, 384), np.float32)
    for g in range(2):
        for a in range(4):
            masks[g, a, :, 32 * a : 32 * a + 32] = 1.0
            masks[g, a, :, 128 + 32 * a : 128 + 32 * a + 32] = 1.0
            masks[g, a, :, 256 + 64 * g + 16 * a : 256 + 64 * g + 16 * a + 16] = 1.0
    masks = masks.reshape(2, 512, 384)
    return (
        jnp.asarray(perm, BF16),
        jnp.asarray(gather, BF16),
        jnp.asarray(spread, BF16),
        jnp.asarray(tile, F32),
        jnp.asarray(rope, F32),
        jnp.asarray(masks, BF16),
    )


def dot(a, b, **kw):
    return jnp.dot(a, b, preferred_element_type=F32, **kw)


def kernel(
    hidden, steps, table, wqkv, wout, q_gain, k_gain, perm_h, gather_h, spread_h, tile_h, rope_h, masks_h,
    out,
    eo, oc, wq_v, wo_v, x_v, table_v, tab, onehot, perm, gather, spread, tile, rope, masks, gain_v,
    modul, turned, normed, nb, xp, qf, rf, qk, vb, vp, attp, delta, upd,
    send, recv, local,
):
    band = lax.axis_index("band")
    frame = lax.axis_index("frame")
    c = lax.rem(band, 2)
    y = lax.rem(band // 2, 8)
    par = lax.rem(y, 2)
    z_lo = lax.rem(frame, 4)
    x = frame // 4
    z = (band // 16) * 4 + z_lo

    def device(dx, dy, dz, core):
        xx = lax.rem(x + dx + 4, 4)
        yy = lax.rem(y + dy + 8, 8)
        zz = lax.rem(z + dz + 8, 8)
        return ((zz // 4) * 16 + yy * 2 + core, xx * 4 + lax.rem(zz, 4))

    y_up, y_dn = device(0, 1, 0, c), device(0, -1, 0, c)
    sib = device(0, 0, 0, 1 - c)

    def shard(ax, i, j):
        xx = lax.rem(x + i * ax + j * (1 - ax) + 4, 4)
        zz = lax.rem(z_lo + i * (1 - ax) + j * ax + 4, 4)
        return xx * 4 + zz

    def fetch(src, dst, k):
        cp = pltpu.make_async_copy(src, dst, local.at[k])
        cp.start()
        return cp

    got_w = [fetch(wqkv, wq_v, 0), fetch(wout, wo_v, 1)]
    own = pl.ds(pl.multiple_of(frame * TOK, TOK), TOK)
    got_own = fetch(hidden.at[own], x_v.at[own], 2)
    got_tab = fetch(table, table_v, 3)
    got_rest = [
        fetch(a, b, 4 + k)
        for k, (a, b) in enumerate(
            ((perm_h, perm), (gather_h, gather), (spread_h, spread), (tile_h, tile), (rope_h, rope), (masks_h, masks), (q_gain, gain_v.at[0]), (k_gain, gain_v.at[1]))
        )
    ]

    barrier = pltpu.get_barrier_semaphore()

    def greet(d):
        pl.semaphore_signal(barrier, inc=1, device_id=d, device_id_type=MESH)

    for move in ((1, 0, 0), (-1, 0, 0), (0, 1, 0), (0, -1, 0), (0, 0, 1), (0, 0, -1)):
        greet(device(*move, c))
    greet(sib)
    for k in range(1, NF):
        greet((band, lax.rem(frame + k, NF)))

    @pl.when(jnp.logical_and(frame == 0, band > 0))
    def _():
        for k in range(NF):
            greet((band - 1, k))

    for cp in got_w:
        cp.wait()
    me = frame
    rest = wq_v[64:72, :].astype(F32)
    rest_o = wo_v[64:72, :].astype(F32)
    tails = (
        jnp.concatenate([rest[:, 0:D], rest[:, D : 2 * D]], axis=0).astype(BF16),
        jnp.concatenate([rest[:, 2 * D :], rest_o], axis=0).astype(BF16),
    )
    for cc in range(2):
        for m in range(2):
            eo[m, cc, me, 0:32, :] = wq_v[32 * cc : 32 * cc + 32, m * D : (m + 1) * D]
            eo[m, cc, me, 32:48, :] = tails[cc]
            eo[m, cc, me, 48:64, :] = wq_v[32 * cc + 16 * m : 32 * cc + 16 * m + 16, 2 * D :]
            oc[m, cc, me] = wo_v[32 * cc + 16 * m : 32 * cc + 16 * m + 16, :]

    pl.semaphore_wait(barrier, 22 + lax.min(NB - 1 - band, 1))

    def push(src, dst, d, ssem, rsem):
        pltpu.make_async_remote_copy(src, dst, send.at[ssem], recv.at[rsem], device_id=d, device_id_type=MESH).start()

    def settle(ref, ssem=None, rsem=None):
        cp = pltpu.make_async_remote_copy(ref, ref, send.at[ssem or 0], recv.at[rsem or 0], device_id=sib, device_id_type=MESH)
        if rsem is None:
            cp.wait_send()
        else:
            cp.wait_recv()

    SPAN = {"E": (0, 48), "F": (48, 16), "YE": (0, 32), "YF": (48, 16), "C": (0, 16), "YC": (0, 16)}

    def block(kind, i, j):
        which = shard(FIRST_X[kind[-1]], i, j)
        m = 1 - par if kind[0] == "Y" else par
        if kind[-1] == "C":
            return oc.at[m, c, which]
        start, size = SPAN[kind]
        return eo.at[m, c, which, pl.ds(start, size)]

    def same_bytes(count, kind):
        return eo.at[0, 0, pl.ds(0, count), pl.ds(0, SPAN[kind][1])]

    def hop_of(i, j):
        return [n for n, hop in enumerate(HOPS) if (i, j) in hop][0]

    def slot(kind, i, j):
        if kind == "E":
            return 4 * i + j + 5
        return 16 + 4 * (KINDS.index(kind) - 1) + hop_of(i, j)

    SIB, HID, HOT, FIN = 36, 42, 43, 44

    def push_block(kind, i, j, d, ri, rj):
        ref = block(kind, i, j)
        push(ref, ref, d, KINDS.index(kind), slot(kind, ri, rj))

    FIRST_X = {"E": 1 - c, "F": 1 - c, "C": 0}

    def ways(kind):
        ax = FIRST_X[kind]
        return device(ax, 0, 1 - ax, c), device(-ax, 0, ax - 1, c), device(1 - ax, 0, ax, c), device(ax - 1, 0, -ax, c)

    WAYS = {kind: ways(kind) for kind in FIRST_X}

    def start_own(kind):
        a_up, a_dn, b_up, b_dn = WAYS[kind]
        push_block(kind, 0, 0, b_up, 0, -1)
        push_block(kind, 0, 0, b_dn, 0, 1)
        push_block(kind, 0, 0, a_up, -1, 0)
        push_block(kind, 0, 0, a_dn, 1, 0)

    turn = [0]

    def forward(kind, i, j):
        if kind[0] != "Y":
            a_up, a_dn, b_up, b_dn = WAYS[kind]
            if j == 0:
                if kind != "C" and i == -1:
                    push_block(kind, i, j, a_up, 2, 0)
                if kind == "C" and i == 1:
                    push_block(kind, i, j, a_dn, 2, 0)
                push_block(kind, i, j, b_up, i, -1)
                push_block(kind, i, j, b_dn, i, 1)
            elif j == -1 and i in (0, -1):
                push_block(kind, i, j, b_up, i, 2)
            elif j == 1 and i in (1, 2):
                push_block(kind, i, j, b_dn, i, 2)
            ref = block(kind, i, j)
            if kind == "E":
                ref = eo.at[par, c, shard(FIRST_X[kind], i, j), pl.ds(0, 32)]
            other = "Y" + kind
            push(ref, ref, y_up if turn[0] % 2 == 0 else y_dn, KINDS.index(other), slot(other, i, j))
            turn[0] += 1
        ref = block(kind, i, j)
        push(ref, ref, sib, 6 + KINDS.index(kind), SIB + KINDS.index(kind))

    def take(kind, hop, hidden_after):
        blocks = HOPS[hop]
        if kind != "E":
            settle(same_bytes(len(blocks), kind), rsem=slot(kind, *blocks[0]))
        for i, j in blocks:
            if kind == "E":
                settle(block(kind, i, j), rsem=slot(kind, i, j))
            forward(kind, i, j)
            send_hidden(hidden_after)

    def from_sibling(kinds):
        for kind in kinds:
            settle(same_bytes(NF - 1, kind), rsem=SIB + KINDS.index(kind))

    step = steps[0, 0]
    lanes = lax.broadcasted_iota(jnp.int32, (8, 128), 1)
    onehot[frame] = (lanes == step).astype(F32)
    def send_onehots():
        for k in range(1, NF):
            to = lax.rem(frame + k, NF)
            push(onehot.at[frame], onehot.at[frame], (band, to), 13, HOT)

    todo = [8, 7, 9, 6, 10, 5, 11, 4, 12, 3, 13, 2, 14, 1, 15]

    def send_hidden(count):
        for _ in range(min(count, len(todo))):
            to = lax.rem(frame + todo.pop(0), NF)
            rows = pl.ds(pl.multiple_of(to * TOK, TOK), TOK)
            push(hidden.at[rows], x_v.at[own], (band, to), 12, HID)

    NT = 384

    def project(dst, lhs, rhs):
        def one(n, _):
            cols = pl.ds(pl.multiple_of(n * NT, NT), NT)
            dst[:, cols] = dot(lhs(), jnp.concatenate([r(cols) for r in rhs], axis=0)).astype(dst.dtype)
            return 0

        lax.fori_loop(0, D // NT, one, 0)

    def piece(m, cc, lo):
        return lambda cols: eo[m, cc, :, lo : lo + 16, cols].reshape(256, NT)

    factor = math.log2(math.e) / math.sqrt(HD)

    def work_tab():
        got_tab.wait()
        tab[...] = jnp.zeros_like(tab)
        for j in range(3):
            tab[j, 0:STEPS, :] = table_v[j]

    def work_mod():
        settle(onehot.at[pl.ds(0, NF - 1)], rsem=HOT)
        oh = onehot[...].reshape(128, 128)
        for j in range(3):
            modul[j] = dot(oh, tab[j], precision=lax.Precision.HIGHEST)

    def work_rope():
        for cp in got_rest:
            cp.wait()
        for m in range(2):
            g = dot(jnp.broadcast_to(gain_v[m], (8, HD)), tile[...], precision=lax.Precision.HIGHEST)
            if m == 0:
                g = g * factor
            rolled = (g, pltpu.roll(g, D - HD // 2, 1), pltpu.roll(g, HD // 2, 1))
            for j in range(3):
                turned[m, j] = rope[j] * rolled[j][0:1, :]

    def norm_frame(f, _):
        r16 = pl.ds(pl.multiple_of(f * TOK, TOK), TOK)
        r8 = pl.multiple_of(f * 8, 8)
        v = x_v[r16, :].astype(F32)
        mean = jnp.mean(v, axis=-1, keepdims=True)
        cen = v - mean
        var = jnp.mean(cen * cen, axis=-1, keepdims=True)
        cen = cen * lax.rsqrt(var + 1e-06)
        scale = 1.0 + modul[1, pl.ds(r8, 8), :]
        shift = modul[0, pl.ds(r8, 8), :]
        normed[pl.ds(r8, 8), :] = cen[0:8] * scale + shift
        normed[pl.ds(pl.multiple_of(r8 + 128, 8), 8), :] = cen[8:16] * scale + shift
        return 0

    def work_ln():
        got_own.wait()
        settle(x_v.at[pl.ds(0, ROWS - TOK)], rsem=HID)
        lax.fori_loop(0, NF, norm_frame, 0, unroll=4)
        nb[...] = normed[...].astype(BF16)

    def work_permute(n):
        cols = pl.ds(n * 512, 512)
        xp[:, cols] = dot(nb[...], perm[:, cols]).astype(BF16)

    def work_multiply(m, kind):
        from_sibling((kind,))
        last = pl.ds(pl.multiple_of(LO0 + KREM * m, KREM), KREM)
        project(
            qf,
            lambda: jnp.concatenate([xp[:, 0:KMAIN], xp[:, last]], axis=1),
            [piece(m, cc, 16 * half) for half in range(2) for cc in range(2)] + [piece(par, 0, 32)],
        )

    def work_stats():
        squares = qf[...]
        ss = dot((squares * squares).astype(BF16), gather[...])
        r = lax.rsqrt(ss * (1.0 / HD) + 1e-06)
        hi = r.astype(BF16)
        lo = (r - hi.astype(F32)).astype(BF16)
        rf[...] = dot(jnp.concatenate([hi, lo], axis=1), jnp.concatenate([spread[...], spread[...]], axis=0))

    def work_turn(m):
        def turn_rows(g, _):
            r32 = pl.ds(pl.multiple_of(g * 32, 32), 32)
            t32 = pl.ds(pl.multiple_of(lax.rem(g, 4) * 32, 32), 32)
            v = qf[r32, :] * rf[r32, :]
            w = v * turned[m, 0, t32, :]
            w = w + pltpu.roll(v, D - HD // 2, 1) * turned[m, 1, t32, :]
            w = w + pltpu.roll(v, HD // 2, 1) * turned[m, 2, t32, :]
            qk[m, r32, :] = w.astype(BF16)
            return 0

        lax.fori_loop(0, ROWS // 32, turn_rows, 0, unroll=2)

    def work_values():
        from_sibling(("F", "YF"))
        project(
            vb,
            lambda: xp[:, 0 : KMAIN + KREM],
            [piece(m, cc, 48) for m in range(2) for cc in range(2)] + [piece(par, 1, 32)],
        )

    def work_permute_values():
        vp[:, 0:512] = dot(vb[...], perm[:, O0 : O0 + 512]).astype(BF16)
        vp[:, 512:1024] = dot(vb[...], perm[:, O0 + 512 : O0 + 1024]).astype(BF16)
        vp[:, 1024:1280] = dot(vb[...], perm[:, HI0 : HI0 + KREM]).astype(BF16)

    def work_attend(h):
        same = (
            lax.rem(lax.broadcasted_iota(jnp.int32, (128, 128), 0), 8)
            == lax.rem(lax.broadcasted_iota(jnp.int32, (128, 128), 1), 8)
        ).astype(F32)
        rows = pl.ds(h * 128, 128)
        num_rem = den_rem = None
        for g in range(4):
            probs = []
            for a in range(4):
                hd = 4 * g + a
                w = (HD * hd) // 128 * 128
                width = min(256, D - w)
                lane = lax.broadcasted_iota(jnp.int32, (16, width), 1) + w
                pick = jnp.logical_and(lane >= HD * hd, lane < HD * (hd + 1)).astype(F32).astype(BF16)
                pick = jnp.concatenate([pick] * 8, axis=0)
                kw = qk[1, rows, w : w + width] * pick
                sc = lax.dot_general(qk[0, rows, w : w + width], kw, (((1,), (1,)), ((), ())), preferred_element_type=F32)
                probs.append((jnp.exp2(sc) * same).astype(BF16))
            p4 = jnp.concatenate(probs, axis=1)
            vg = jnp.concatenate([
                vp[rows, g * 128 : g * 128 + 128],
                vp[rows, 512 + g * 128 : 512 + g * 128 + 128],
                vp[rows, 1024 + (g // 2) * 128 : 1024 + (g // 2) * 128 + 128],
            ], axis=1)
            mk = masks[g % 2]
            num = dot(p4, jnp.concatenate([vg] * 4, axis=0) * mk)
            den = dot(p4, mk)
            inv = 1.0 / den[:, 0:128]
            attp[rows, g * 128 : g * 128 + 128] = (num[:, 0:128] * inv).astype(BF16)
            attp[rows, 512 + g * 128 : 512 + g * 128 + 128] = (num[:, 128:256] * inv).astype(BF16)
            if g % 2 == 0:
                num_rem, den_rem = num[:, 256:384], den[:, 256:384]
            else:
                lo = 1024 + (g // 2) * 128
                attp[rows, lo : lo + 128] = ((num_rem + num[:, 256:384]) / (den_rem + den[:, 256:384])).astype(BF16)

    work = {
        "tab": work_tab,
        "mod": work_mod,
        "rope": work_rope,
        "ln": work_ln,
        "p0": lambda: work_permute(0),
        "p1": lambda: work_permute(1),
        "p2": lambda: work_permute(2),
        "f0": lambda: work_multiply(par, "E"),
        "f1": work_stats,
        "f2": lambda: work_turn(par),
        "g0": lambda: work_multiply(1 - par, "YE"),
        "g1": work_stats,
        "g2": lambda: work_turn(1 - par),
        "v": work_values,
        "vp": work_permute_values,
        "a0": lambda: work_attend(0),
        "a1": lambda: work_attend(1),
    }

    send_onehots()
    for name, hop, *more in SCHEDULE:
        if name in work:
            work[name]()
        elif name not in KINDS:
            send_hidden(name)
        elif hop < 0:
            start_own(name)
        else:
            take(name, hop, more[0] if more else 0)

    from_sibling(("C", "YC"))

    def o_rows(cc):
        return lambda cols: jnp.concatenate([oc[0, cc, :, :, cols], oc[1, cc, :, :, cols]], axis=1).reshape(512, NT)

    project(delta, lambda: attp[...], [o_rows(0), o_rows(1), piece(par, 1, 32)])

    for k in range(NF):
        f = lax.rem(frame + k, NF)
        r16 = pl.ds(pl.multiple_of(f * TOK, TOK), TOK)
        r8 = pl.multiple_of(f * 8, 8)
        gate = modul[2, pl.ds(r8, 8), :]
        both = jnp.concatenate([
            gate * delta[pl.ds(r8, 8), :],
            gate * delta[pl.ds(pl.multiple_of(r8 + 128, 8), 8), :],
        ], axis=0)
        upd[r16, :] = (x_v[r16, :].astype(F32) + both).astype(BF16)
        to_band = band + f // (NF - 1)
        goes = to_band < NB
        if k == NF - 1:
            goes = jnp.logical_and(goes, frame == 0)
            stay = pltpu.make_async_copy(upd.at[r16], out.at[own], local.at[0])

            @pl.when(frame > 0)
            def _():
                stay.start()
                stay.wait()

        pl.when(goes)(functools.partial(push, upd.at[r16], out.at[own], (to_band, lax.rem(f + 1, NF)), 14, FIN))

    some, most = pl.ds(0, ROWS - 2 * TOK), pl.ds(0, ROWS - TOK)
    starts, ends = frame == 0, band == NB - 1
    both_ways = jnp.logical_and
    pl.when(both_ways(starts, band > 0))(lambda: settle(out, rsem=FIN))
    pl.when(frame > 0)(lambda: settle(out.at[most], rsem=FIN))
    pl.when(both_ways(starts, band < NB - 1))(lambda: settle(upd, ssem=14))
    pl.when(starts == ends)(lambda: settle(upd.at[most], ssem=14))
    pl.when(both_ways(frame > 0, ends))(lambda: settle(upd.at[some], ssem=14))
    settle(hidden.at[most], ssem=12)
    settle(onehot.at[pl.ds(0, NF - 1)], ssem=13)
    for n, kind in enumerate(KINDS):
        settle(same_bytes(NF - 1, kind), ssem=n)
        settle(same_bytes(NF - 1, kind), ssem=6 + n)


def local_step(hidden, timesteps, ada_table, w_qkv, w_out, q_gain, k_gain, fresh):
    hbm = pl.BlockSpec(memory_space=pl.ANY)
    consts = constants()
    shapes = [
        pltpu.VMEM((2, 2, 16, 64, D), BF16),
        pltpu.VMEM((2, 2, 16, 16, D), BF16),
        pltpu.VMEM((72, 3 * D), BF16),
        pltpu.VMEM((72, D), BF16),
        pltpu.VMEM((ROWS, D), BF16),
        pltpu.VMEM((3, STEPS, D), F32),
        pltpu.VMEM((3, 128, D), F32),
        pltpu.VMEM((NF, 8, 128), F32),
        *[pltpu.VMEM(a.shape, a.dtype) for a in consts],
        pltpu.VMEM((2, 1, HD), F32),
        pltpu.VMEM((3, 128, D), F32),
        pltpu.VMEM((2, 3, 128, D), F32),
        pltpu.VMEM((ROWS, D), F32),
        pltpu.VMEM((ROWS, D), BF16),
        pltpu.VMEM((ROWS, O0), BF16),
        pltpu.VMEM((ROWS, D), F32),
        pltpu.VMEM((ROWS, D), F32),
        pltpu.VMEM((2, ROWS, D), BF16),
        pltpu.VMEM((ROWS, D), BF16),
        pltpu.VMEM((ROWS, 1280), BF16),
        pltpu.VMEM((ROWS, 1280), BF16),
        pltpu.VMEM((ROWS, D), F32),
        pltpu.VMEM((ROWS, D), BF16),
        pltpu.SemaphoreType.DMA((15,)),
        pltpu.SemaphoreType.DMA((45,)),
        pltpu.SemaphoreType.DMA((12,)),
    ]
    moved = pl.pallas_call(
        kernel,
        out_shape=jax.ShapeDtypeStruct((ROWS, D), BF16),
        in_specs=[hbm, pl.BlockSpec(memory_space=pltpu.SMEM)] + [hbm] * (5 + len(consts)),
        out_specs=hbm,
        scratch_shapes=shapes,
        compiler_params=pltpu.CompilerParams(collective_id=0, has_side_effects=True, vmem_limit_bytes=56 << 20),
        name="queue_step",
    )(hidden[0, 0], timesteps, jnp.transpose(ada_table, (1, 0, 2)), w_qkv, w_out, q_gain[None], k_gain[None], *consts)
    first = jnp.logical_and(lax.axis_index("band") == 0, lax.axis_index("frame") == 0)
    return jnp.where(first, fresh, moved)[None, None]


def solution(mesh):
    return jax.shard_map(
        local_step,
        mesh=mesh,
        in_specs=(
            P("band", "frame", None, None),
            P("band", "frame"),
            P(),
            P("frame", None),
            P("frame", None),
            P(),
            P(),
            P(),
        ),
        out_specs=P("band", "frame", None, None),
        check_vma=False,
    )
```

time: 87.2 us -> 75.8 us (0.87)
  Pallas kernels: 84.3 us -> 72.9 us
    pallas_call x1, Pallas kernels: 84.3 us -> 72.9 us  [local_step(): pl.pallas_call(kernel, out_shape=jax.ShapeDtypeStruct((ROWS, D), BF16), i...]
where the time goes in v2:
time: 75.8 us; the launch traced here: 75.6 us
  Pallas kernels  72.9 us (96%)
  other arithmetic  1.96 us (3%)
    pallas_call x1, Pallas kernels, local_step(): pl.pallas_call(kernel, out_shape=jax.ShapeDtypeStruct((ROWS, D), BF16), i...  72.9 us
    broadcast_in_dim x1, other arithmetic, local_step(): return jnp.where(first, fresh, moved)[None, None]  1.96 us

profile of v2, /device:TPU:1, one launch (start us, length us, event | category | flops | bytes accessed | tf_op | source)
XLA Modules:
  0.0 75.6 jit_solution(1831076825887723297)
XLA Ops:
  0.0 0.0 copy-start
  0.7 72.9 %queue_step.1 = bf16[256,1152]{1,0:T(8,128)(2,1)} custom-call(bf16[256,1152]{1,0:T(8,128)(2,1)} %bitcast.6, s32[1,1]{1,0:T(1,128)S(6)} %copy.15.steps, f32[3,30,1152]{2,1,0:T(8,128)} %bitcast.7, bf16[72,3456]{1,0:T(8,128)(2,1)} %wqkv.1, bf16[72,1152]{1,0:T(8,128)(2,1)} %wout.1, f32[1,72]{1,0:T(1,128)} %bitcast.8, f32[1,72]{1,0:T(1,128)} %bitcast.9, ...), custom_call_target="tpu_custom_call" | custom-call | tf_op jit(solution)/shard_map/queue_step/pallas_call | solution.py:526
  73.6 0.0 copy-done
  73.7 2.0 %select_bitcast_fusion = bf16[1,1,256,1152]{3,2,1,0:T(8,128)(2,1)} fusion(bf16[256,1152]{1,0:T(8,128)(2,1)S(1)} %copy-done, bf16[256,1152]{1,0:T(8,128)(2,1)} %queue_step.1, pred[]{:T(512)S(6)} %and.5), kind=kLoop, calls=%fused_computation | loop fusion | flops 294912 | bytes 1769473 | tf_op jit(solution)/shard_map/broadcast_in_dim | solution.py:536
Async XLA Ops:
  0.0 73.6 %copy-start = (bf16[256,1152]{1,0:T(8,128)(2,1)S(1)}, bf16[256,1152]{1,0:T(8,128)(2,1)}, u32[]{:S(2)}) copy-start(bf16[256,1152]{1,0:T(8,128)(2,1)} %param.21) | copy-start | bytes 1769476

commit v3 on v2

--- a/solution.py
+++ b/solution.py
@@ -25,11 +25,11 @@
     ((2, 2),),
 )
 SCHEDULE = (
-    ("E", -1), (3, 0), ("F", -1), ("C", -1), ("E", 0, 1), ("tab", 0), ("mod", 0), ("rope", 0),
-    ("F", 0), ("C", 0), ("E", 1, 1), ("F", 1), ("C", 1), ("E", 2, 1), ("YE", 0), ("F", 2),
-    ("C", 2), ("E", 3), ("YE", 1), ("F", 3), ("ln", 0), ("YE", 2), ("p0", 0), ("YF", 0),
-    ("YF", 1), ("YC", 0), ("p1", 0), ("YE", 3), ("p2", 0), ("C", 3), ("f0", 0), ("YF", 2),
-    ("YF", 3), ("f1", 0), ("f2", 0), ("YC", 1), ("g0", 0), ("g1", 0), ("g2", 0), ("YC", 2),
+    ("E", -1), (3, 0), ("F", -1), ("E", 0, 1), ("tab", 0), ("mod", 0), ("rope", 0), ("F", 0),
+    ("C", -1), ("E", 1, 1), ("F", 1), ("C", 0), ("E", 2, 1), ("YE", 0), ("F", 2), ("C", 1),
+    ("E", 3), ("YE", 1), ("F", 3), ("C", 2), ("ln", 0), ("YE", 2), ("p0", 0), ("YF", 0),
+    ("YF", 1), ("YC", 0), ("p1", 0), ("YE", 3), ("p2", 0), ("f0", 0), ("C", 3), ("YF", 2),
+    ("YF", 3), ("f1", 0), ("f2", 0), ("YC", 1), ("g0", 0), ("YC", 2), ("g1", 0), ("g2", 0),
     ("v", 0), ("YC", 3), ("vp", 0), ("a0", 0), ("a1", 0),
 )
 
@@ -266,23 +266,24 @@
             to = lax.rem(frame + k, NF)
             push(onehot.at[frame], onehot.at[frame], (band, to), 13, HOT)
 
-    todo = [8, 7, 9, 6, 10, 5, 11, 4, 12, 3, 13, 2, 14, 1, 15]
+    far_first = [(dx, dz) for dz in (2, 3, 1, 0) for dx in (2, 1, 3, 0)]
+    todo = far_first[:-1]
+
+    def partner(dx, dz):
+        return lax.rem(x + dx, 4) * 4 + lax.rem(z_lo + dz, 4)
+
 
     def send_hidden(count):
         for _ in range(min(count, len(todo))):
-            to = lax.rem(frame + todo.pop(0), NF)
+            to = partner(*todo.pop(0))
             rows = pl.ds(pl.multiple_of(to * TOK, TOK), TOK)
             push(hidden.at[rows], x_v.at[own], (band, to), 12, HID)
 
-    NT = 384
+    NT = D
 
     def project(dst, lhs, rhs):
-        def one(n, _):
-            cols = pl.ds(pl.multiple_of(n * NT, NT), NT)
-            dst[:, cols] = dot(lhs(), jnp.concatenate([r(cols) for r in rhs], axis=0)).astype(dst.dtype)
-            return 0
-
-        lax.fori_loop(0, D // NT, one, 0)
+        cols = pl.ds(0, NT)
+        dst[...] = dot(lhs(), jnp.concatenate([r(cols) for r in rhs], axis=0)).astype(dst.dtype)
 
     def piece(m, cc, lo):
         return lambda cols: eo[m, cc, :, lo : lo + 16, cols].reshape(256, NT)
@@ -329,7 +330,7 @@
     def work_ln():
         got_own.wait()
         settle(x_v.at[pl.ds(0, ROWS - TOK)], rsem=HID)
-        lax.fori_loop(0, NF, norm_frame, 0, unroll=4)
+        lax.fori_loop(0, NF, norm_frame, 0, unroll=8)
         nb[...] = normed[...].astype(BF16)
 
     def work_permute(n):
@@ -454,8 +455,9 @@
 
     project(delta, lambda: attp[...], [o_rows(0), o_rows(1), piece(par, 1, 32)])
 
-    for k in range(NF):
-        f = lax.rem(frame + k, NF)
+    for place in far_first:
+        to_frame = partner(*place)
+        f = lax.rem(to_frame + NF - 1, NF)
         r16 = pl.ds(pl.multiple_of(f * TOK, TOK), TOK)
         r8 = pl.multiple_of(f * 8, 8)
         gate = modul[2, pl.ds(r8, 8), :]
@@ -466,7 +468,7 @@
         upd[r16, :] = (x_v[r16, :].astype(F32) + both).astype(BF16)
         to_band = band + f // (NF - 1)
         goes = to_band < NB
-        if k == NF - 1:
+        if place == (0, 0):
             goes = jnp.logical_and(goes, frame == 0)
             stay = pltpu.make_async_copy(upd.at[r16], out.at[own], local.at[0])
 
@@ -475,7 +477,7 @@
                 stay.start()
                 stay.wait()
 
-        pl.when(goes)(functools.partial(push, upd.at[r16], out.at[own], (to_band, lax.rem(f + 1, NF)), 14, FIN))
+        pl.when(goes)(functools.partial(push, upd.at[r16], out.at[own], (to_band, to_frame), 14, FIN))
 
     some, most = pl.ds(0, ROWS - 2 * TOK), pl.ds(0, ROWS - TOK)
     starts, ends = frame == 0, band == NB - 1

time: 75.8 us -> 72.6 us (0.958)
  Pallas kernels: 72.9 us -> 69.8 us
    pallas_call x1, Pallas kernels: 72.9 us -> 69.8 us  [local_step(): pl.pallas_call(kernel, out_shape=jax.ShapeDtypeStruct((ROWS, D), BF16), i...]
where the time goes in v3:
time: 72.6 us; the launch traced here: 72.4 us
  Pallas kernels  69.8 us (96%)
  other arithmetic  1.96 us (3%)
  between operations  0.73 us (1%)
    pallas_call x1, Pallas kernels, local_step(): pl.pallas_call(kernel, out_shape=jax.ShapeDtypeStruct((ROWS, D), BF16), i...  69.8 us
    broadcast_in_dim x1, other arithmetic, local_step(): return jnp.where(first, fresh, moved)[None, None]  1.96 us

profile of v3, /device:TPU:1, one launch (start us, length us, event | category | flops | bytes accessed | tf_op | source)
XLA Modules:
  0.0 72.4 jit_solution(4550637482329739624)
XLA Ops:
  0.0 0.0 copy-start
  0.7 69.8 %queue_step.1 = bf16[256,1152]{1,0:T(8,128)(2,1)} custom-call(bf16[256,1152]{1,0:T(8,128)(2,1)} %bitcast.6, s32[1,1]{1,0:T(1,128)S(6)} %copy.15.steps, f32[3,30,1152]{2,1,0:T(8,128)} %bitcast.7, bf16[72,3456]{1,0:T(8,128)(2,1)} %wqkv.1, bf16[72,1152]{1,0:T(8,128)(2,1)} %wout.1, f32[1,72]{1,0:T(1,128)} %bitcast.8, f32[1,72]{1,0:T(1,128)} %bitcast.9, ...), custom_call_target="tpu_custom_call" | custom-call | tf_op jit(solution)/shard_map/queue_step/pallas_call | solution.py:528
  70.5 0.0 copy-done
  70.5 2.0 %select_bitcast_fusion = bf16[1,1,256,1152]{3,2,1,0:T(8,128)(2,1)} fusion(bf16[256,1152]{1,0:T(8,128)(2,1)S(1)} %copy-done, bf16[256,1152]{1,0:T(8,128)(2,1)} %queue_step.1, pred[]{:T(512)S(6)} %and.5), kind=kLoop, calls=%fused_computation | loop fusion | flops 294912 | bytes 1769473 | tf_op jit(solution)/shard_map/broadcast_in_dim | solution.py:538
Async XLA Ops:
  0.0 70.5 %copy-start = (bf16[256,1152]{1,0:T(8,128)(2,1)S(1)}, bf16[256,1152]{1,0:T(8,128)(2,1)}, u32[]{:S(2)}) copy-start(bf16[256,1152]{1,0:T(8,128)(2,1)} %param.21) | copy-start | bytes 1769476

commit v4 on v3

--- a/solution.py
+++ b/solution.py
@@ -25,12 +25,12 @@
     ((2, 2),),
 )
 SCHEDULE = (
-    ("E", -1), (3, 0), ("F", -1), ("E", 0, 1), ("tab", 0), ("mod", 0), ("rope", 0), ("F", 0),
-    ("C", -1), ("E", 1, 1), ("F", 1), ("C", 0), ("E", 2, 1), ("YE", 0), ("F", 2), ("C", 1),
-    ("E", 3), ("YE", 1), ("F", 3), ("C", 2), ("ln", 0), ("YE", 2), ("p0", 0), ("YF", 0),
-    ("YF", 1), ("YC", 0), ("p1", 0), ("YE", 3), ("p2", 0), ("f0", 0), ("C", 3), ("YF", 2),
-    ("YF", 3), ("f1", 0), ("f2", 0), ("YC", 1), ("g0", 0), ("YC", 2), ("g1", 0), ("g2", 0),
-    ("v", 0), ("YC", 3), ("vp", 0), ("a0", 0), ("a1", 0),
+    ("E", -1), ("F", -1), ("C", -1), (3, 0), ("E", 0, 1), ("F", 0), ("C", 0), ("tab", 0),
+    ("mod", 0), ("E", 1, 1), ("YE", 0), ("F", 1), ("YF", 0), ("C", 1), ("YC", 0), ("rope", 0),
+    ("E", 2, 1), ("F", 2), ("C", 2), ("YE", 1), ("YF", 1), ("YC", 1), ("E", 3), ("F", 3),
+    ("C", 3), ("ln", 0), ("YE", 2), ("p0", 0), ("YF", 2), ("YC", 2), ("p1", 0), ("YE", 3),
+    ("p2", 0), ("YF", 3), ("YC", 3), ("f0", 0), ("f1", 0), ("f2", 0), ("g0", 0), ("g1", 0),
+    ("g2", 0), ("v", 0), ("vp", 0), ("a0", 0), ("a1", 0),
 )
 
 
@@ -129,7 +129,7 @@
     got_rest = [
         fetch(a, b, 4 + k)
         for k, (a, b) in enumerate(
-            ((perm_h, perm), (gather_h, gather), (spread_h, spread), (tile_h, tile), (rope_h, rope), (masks_h, masks), (q_gain, gain_v.at[0]), (k_gain, gain_v.at[1]))
+            ((tile_h, tile), (rope_h, rope), (q_gain, gain_v.at[0]), (k_gain, gain_v.at[1]), (perm_h, perm), (gather_h, gather), (spread_h, spread), (masks_h, masks))
         )
     ]
 
@@ -303,7 +303,7 @@
             modul[j] = dot(oh, tab[j], precision=lax.Precision.HIGHEST)
 
     def work_rope():
-        for cp in got_rest:
+        for cp in got_rest[:4]:
             cp.wait()
         for m in range(2):
             g = dot(jnp.broadcast_to(gain_v[m], (8, HD)), tile[...], precision=lax.Precision.HIGHEST)
@@ -328,6 +328,8 @@
         return 0
 
     def work_ln():
+        for cp in got_rest[4:]:
+            cp.wait()
         got_own.wait()
         settle(x_v.at[pl.ds(0, ROWS - TOK)], rsem=HID)
         lax.fori_loop(0, NF, norm_frame, 0, unroll=8)

time: 72.6 us -> 71.9 us (level)
  no operation moved by 1% of the time
where the time goes in v4:
time: 71.9 us; the launch traced here: 71.8 us
  Pallas kernels  69.1 us (96%)
  other arithmetic  1.96 us (3%)
  between operations  0.73 us (1%)
    pallas_call x1, Pallas kernels, local_step(): pl.pallas_call(kernel, out_shape=jax.ShapeDtypeStruct((ROWS, D), BF16), i...  69.1 us
    broadcast_in_dim x1, other arithmetic, local_step(): return jnp.where(first, fresh, moved)[None, None]  1.96 us

profile of v4, /device:TPU:1, one launch (start us, length us, event | category | flops | bytes accessed | tf_op | source)
XLA Modules:
  0.0 71.8 jit_solution(5061937521193449283)
XLA Ops:
  0.0 0.0 copy-start
  0.7 69.1 %queue_step.1 = bf16[256,1152]{1,0:T(8,128)(2,1)} custom-call(bf16[256,1152]{1,0:T(8,128)(2,1)} %bitcast.6, s32[1,1]{1,0:T(1,128)S(6)} %copy.15.steps, f32[3,30,1152]{2,1,0:T(8,128)} %bitcast.7, bf16[72,3456]{1,0:T(8,128)(2,1)} %wqkv.1, bf16[72,1152]{1,0:T(8,128)(2,1)} %wout.1, f32[1,72]{1,0:T(1,128)} %bitcast.8, f32[1,72]{1,0:T(1,128)} %bitcast.9, ...), custom_call_target="tpu_custom_call" | custom-call | tf_op jit(solution)/shard_map/queue_step/pallas_call | solution.py:530
  69.8 0.0 copy-done
  69.8 2.0 %select_bitcast_fusion = bf16[1,1,256,1152]{3,2,1,0:T(8,128)(2,1)} fusion(bf16[256,1152]{1,0:T(8,128)(2,1)S(1)} %copy-done, bf16[256,1152]{1,0:T(8,128)(2,1)} %queue_step.1, pred[]{:T(512)S(6)} %and.5), kind=kLoop, calls=%fused_computation | loop fusion | flops 294912 | bytes 1769473 | tf_op jit(solution)/shard_map/broadcast_in_dim | solution.py:540
Async XLA Ops:
  0.0 69.8 %copy-start = (bf16[256,1152]{1,0:T(8,128)(2,1)S(1)}, bf16[256,1152]{1,0:T(8,128)(2,1)}, u32[]{:S(2)}) copy-start(bf16[256,1152]{1,0:T(8,128)(2,1)} %param.21) | copy-start | bytes 1769476
